TPU v7x, 32 devices: a whole 2x2x4 slice. The times are simulated.
32 devices in a mesh: dp: 2 (over core), chan: 4 (over z), seq: 4 (over y, x).
Axes of the slice: x: 2, y: 2, z: 4, core: 2. Of those that a mesh axis runs over, the one named last changes fastest.
Arguments:
- query_proj: bfloat16 [2, 2048, 2048], P('dp', 'chan', 'seq'), may hold values from -6 to 6
- key_proj: bfloat16 [2, 2048, 2048], P('dp', 'chan', 'seq'), may hold values from -6 to 6
- value_proj: bfloat16 [2, 2048, 2048], P('dp', 'chan', 'seq'), may hold values from -6 to 6
- grad_out: bfloat16 [2, 2048, 2048], P('dp', 'chan', 'seq'), may hold values from -6 to 6
- out_weight: bfloat16 [2048, 2048], P('chan'), may hold values from -0.125 to 0.125
- long_filter: float32 [2048, 2048], P(('chan', 'seq')), may hold values from -2 to 2, as said below
Outputs:
- grad_query: bfloat16 [2, 2048, 2048], P('dp', 'chan', 'seq')
- grad_key: bfloat16 [2, 2048, 2048], P('dp', 'chan', 'seq')
- grad_value: bfloat16 [2, 2048, 2048], P('dp', 'chan', 'seq')
- grad_weight: float32 [2048, 2048], P('chan')
Inputs may be any that keep to these rules, and one draw needn't show every extreme that they name: `long_filter`: taps of each channel's causal filter.
All inputs are finite; a program needn't handle non-finite values.
Results may differ from a plain program's by a relative error of at most 0.0029.
Values may be sent and summed in bfloat16 or wider, within the bound.
A program may use at most 64 MiB of HBM per device.

v0:
```python
import math

import jax
import jax.numpy as jnp
from jax import lax
from jax.sharding import PartitionSpec as P

precise = lax.Precision.HIGHEST


def phase_table(row_count, col_count, period):
    row_ids = lax.broadcasted_iota(jnp.int32, (row_count, col_count), 0)
    col_ids = lax.broadcasted_iota(jnp.int32, (row_count, col_count), 1)
    angles = 2.0 * math.pi / period * (row_ids * col_ids % period).astype(jnp.float32)
    return (jnp.cos(angles), jnp.sin(angles))


def make_tables(length):
    total_len = 2 * length
    wide_count = total_len // 128
    half_rows = length // 128
    return (
        phase_table(half_rows, wide_count, wide_count),
        phase_table(wide_count, 128, total_len),
        phase_table(128, 128, 128),
    )


def forward_spectrum(signal, tables):
    (cos_first, sin_first), (cos_twist, sin_twist), (cos_second, sin_second) = tables
    row_count = signal.shape[0]
    half_rows = cos_first.shape[0]
    shaped = signal.reshape(row_count, half_rows, 128)
    real_first = jnp.einsum("mab,ak->mkb", shaped, cos_first, precision=precise)
    imag_first = -jnp.einsum("mab,ak->mkb", shaped, sin_first, precision=precise)
    real_mid = real_first * cos_twist + imag_first * sin_twist
    imag_mid = imag_first * cos_twist - real_first * sin_twist
    real_last = jnp.einsum("mkb,bj->mkj", real_mid, cos_second, precision=precise) + jnp.einsum(
        "mkb,bj->mkj", imag_mid, sin_second, precision=precise
    )
    imag_last = jnp.einsum("mkb,bj->mkj", imag_mid, cos_second, precision=precise) - jnp.einsum(
        "mkb,bj->mkj", real_mid, sin_second, precision=precise
    )
    return (real_last, imag_last)


def inverse_spectrum(real_spec, imag_spec, tables):
    (cos_first, sin_first), (cos_twist, sin_twist), (cos_second, sin_second) = tables
    row_count = real_spec.shape[0]
    half_rows = cos_first.shape[0]
    real_mid = jnp.einsum("mkj,jb->mkb", real_spec, cos_second, precision=precise) - jnp.einsum(
        "mkj,jb->mkb", imag_spec, sin_second, precision=precise
    )
    imag_mid = jnp.einsum("mkj,jb->mkb", real_spec, sin_second, precision=precise) + jnp.einsum(
        "mkj,jb->mkb", imag_spec, cos_second, precision=precise
    )
    real_turn = real_mid * cos_twist - imag_mid * sin_twist
    imag_turn = real_mid * sin_twist + imag_mid * cos_twist
    shaped = jnp.einsum("mkb,ak->mab", real_turn, cos_first, precision=precise) - jnp.einsum(
        "mkb,ak->mab", imag_turn, sin_first, precision=precise
    )
    return shaped.reshape(row_count, half_rows * 128) / (2.0 * half_rows * 128)


def to_full(block_rows):
    return lax.all_to_all(block_rows, "seq", split_axis=1, concat_axis=2, tiled=True)


def to_blocks(whole_rows):
    return lax.all_to_all(whole_rows, "seq", split_axis=2, concat_axis=1, tiled=True)


def shards(query_proj, key_proj, value_proj, grad_out, out_weight, long_filter):
    length = long_filter.shape[1]
    tables = make_tables(length)
    query_vals = query_proj[0].astype(jnp.float32)
    key_vals = key_proj[0].astype(jnp.float32)
    value_vals = value_proj[0].astype(jnp.float32)
    mixed_in = key_vals * value_vals
    mixed_full = to_full(mixed_in[None])[0]
    filt_real, filt_imag = forward_spectrum(long_filter, tables)
    sig_real, sig_imag = forward_spectrum(mixed_full, tables)
    conv_full = inverse_spectrum(
        sig_real * filt_real - sig_imag * filt_imag,
        sig_real * filt_imag + sig_imag * filt_real,
        tables,
    )
    conv_out = to_blocks(conv_full[None])[0]
    gated_out = (query_vals * conv_out).astype(jnp.bfloat16)
    piece_rows = lax.all_gather(grad_out, "chan", axis=1, tiled=True)[0]
    grad_part = jnp.dot(out_weight, piece_rows, preferred_element_type=jnp.float32)
    column_block = lax.dot_general(
        gated_out, piece_rows, (((1,), (1,)), ((), ())), preferred_element_type=jnp.float32
    )
    weight_part = column_block
    grad_mid, weight_part = (grad_part, weight_part)
    weight_total = lax.psum(weight_part, ("dp", "seq"))
    grad_weight = weight_total * (1.0 / math.sqrt(lax.axis_size("dp") * length))
    grad_gate = query_vals * grad_mid
    grad_query = (grad_mid * conv_out).astype(jnp.bfloat16)
    gate_full = to_full(grad_gate[None])[0]
    grad_real, grad_imag = forward_spectrum(gate_full, tables)
    back_full = inverse_spectrum(
        grad_real * filt_real + grad_imag * filt_imag,
        grad_imag * filt_real - grad_real * filt_imag,
        tables,
    )
    grad_mixed = to_blocks(back_full[None])[0]
    grad_key = (grad_mixed * value_vals).astype(jnp.bfloat16)
    grad_value = (grad_mixed * key_vals).astype(jnp.bfloat16)
    return (grad_query[None], grad_key[None], grad_value[None], grad_weight)


def solution(mesh):
    placed = (
        P("dp", "chan", "seq"),
        P("dp", "chan", "seq"),
        P("dp", "chan", "seq"),
        P("dp", "chan", "seq"),
        P("chan", None),
        P(("chan", "seq"), None),
    )
    return jax.shard_map(
        shards,
        mesh=mesh,
        in_specs=placed,
        out_specs=(
            P("dp", "chan", "seq"),
            P("dp", "chan", "seq"),
            P("dp", "chan", "seq"),
            P("chan", None),
        ),
        check_vma=False,
    )
```

profile of v0, /device:TPU:0, one launch (start us, length us, event | category | flops | bytes accessed | tf_op | source)
XLA Modules:
  0.0 288.7 jit_solution(3395104251295786275)
XLA Ops:
  7.9 3.2 %fusion.76 = f32[1,512,512]{2,0,1:T(1,128)} fusion(bf16[1,512,512]{2,1,0:T(8,128)(2,1)} %param.7, bf16[1,512,512]{2,1,0:T(8,128)(2,1)} %param.8), kind=kLoop, calls=%fused_computation.80 | loop fusion | flops 786432 | bytes 2097152 | tf_op jit(solution)/shard_map/mul | solution.py:79
  11.2 5.2 %all-to-all-start = ((f32[1,512,512]{2,0,1:T(1,128)}), f32[1,512,512]{2,0,1:T(1,128)}, u32[]{:S(2)}, u32[]{:S(2)}) async-start(f32[1,512,512]{2,0,1:T(1,128)} %fusion.76), calls=%async_computation | async-start | bytes 2097152 | tf_op jit(solution)/shard_map/all_to_all | solution.py:66
  17.7 40.5 %all-gather.2.cloned.1.call-done = bf16[1,2048,512]{2,1,0:T(8,128)(2,1)} async-done(((bf16[1,512,512]{2,1,0:T(8,128)(2,1)}), bf16[1,2048,512]{2,1,0:T(8,128)(2,1)}) %all-gather.2.cloned.1.call-update) | async-done | bytes 2097168 | tf_op jit(solution)/shard_map/all_gather | solution.py:90
  58.3 2.9 %fusion.2 = f32[512,512]{1,0:T(8,128)S(1)} fusion(bf16[512,2048]{1,0:T(8,128)(2,1)S(1)} %copy-done, bf16[1,2048,512]{2,1,0:T(8,128)(2,1)} %all-gather.2.cloned.1.call-done), kind=kOutput, calls=%fused_computation.2 | convolution fusion | flops 1073741824 | bytes 5242880 | tf_op jit(solution)/shard_map/dot_general | solution.py:91
  64.4 4.1 %all-to-all-start.2 = ((f32[1,512,512]{2,0,1:T(1,128)}), f32[1,512,512]{2,0,1:T(1,128)S(1)}, u32[]{:S(2)}, u32[]{:S(2)}) async-start(f32[1,512,512]{2,0,1:T(1,128)} %copy.89), calls=%async_computation.2 | async-start | bytes 2097152 | tf_op jit(solution)/shard_map/all_to_all | solution.py:66
  68.6 3.2 %fusion.142 = f32[32,128,128]{2,0,1:T(8,128)} fusion(f32[128,16,128]{2,1,0:T(8,128)S(1)} %bitcast.146), kind=kOutput, calls=%fused_computation.135 | convolution fusion | flops 100670464 | bytes 3145728 | tf_op jit(solution)/shard_map/mab,ak->mkb/dot_general | solution.py:35
  71.9 3.2 %fusion.150 = f32[32,128,128]{2,0,1:T(8,128)} fusion(f32[128,16,128]{2,1,0:T(8,128)S(1)} %bitcast.147), kind=kOutput, calls=%fused_computation.143 | convolution fusion | flops 100670464 | bytes 3145728 | tf_op jit(solution)/shard_map/mab,ak->mkb/dot_general | solution.py:34
  77.4 3.2 %fusion.144 = f32[32,128,128]{2,0,1:T(8,128)} fusion(f32[128,16,128]{2,1,0:T(8,128)S(1)} %reshape_squeeze.6), kind=kOutput, calls=%fused_computation.137 | convolution fusion | flops 100670464 | bytes 3145728 | tf_op jit(solution)/shard_map/mab,ak->mkb/dot_general | solution.py:35
  86.8 3.7 %add_bitcast_fusion = (f32[128,32,128]{2,1,0:T(8,128)S(1)}, f32[128,32,128]{2,1,0:T(8,128)S(1)}, f32[128,32,128]{2,1,0:T(8,128)S(1)}, f32[128,32,128]{2,1,0:T(8,...) fusion(f32[32,128,128]{2,0,1:T(8,128)S(1)} %fusion.147, f32[32,128,128]{2,0,1:T(8,128)S(1)} %fusion.139, ...), kind=kOutput, calls=%fused_computation.18 | convolution fusion | flops 111680512 | bytes 24150016 | tf_op jit(solution)/shard_map/mab,ak->mkb/dot_general | solution.py:34
  90.5 3.6 %fusion.30 = f32[128,32,128]{2,0,1:T(8,128)S(1)} fusion(f32[128,32,128]{2,1,0:T(8,128)S(1)} %get-tuple-element.30), kind=kOutput, calls=%fused_computation.45 | convolution fusion | flops 805535744 | bytes 4194304 | tf_op jit(solution)/shard_map/mkb,bj->mkj/dot_general | solution.py:38
  94.1 3.6 %fusion.28 = f32[128,32,128]{2,0,1:T(8,128)S(1)} fusion(f32[128,32,128]{2,1,0:T(8,128)S(1)} %get-tuple-element.30), kind=kOutput, calls=%fused_computation.43 | convolution fusion | flops 805535744 | bytes 4194304 | tf_op jit(solution)/shard_map/mkb,bj->mkj/dot_general | solution.py:41
  97.7 3.8 %fusion.22 = f32[128,32,128]{2,0,1:T(8,128)S(1)} fusion(f32[128,32,128]{2,1,0:T(8,128)S(1)} %get-tuple-element.28), kind=kOutput, calls=%fused_computation.37 | convolution fusion | flops 805535744 | bytes 4194304 | tf_op jit(solution)/shard_map/mkb,bj->mkj/dot_general | solution.py:38
  101.5 3.6 %fusion.20 = f32[128,32,128]{2,0,1:T(8,128)S(1)} fusion(f32[128,32,128]{2,1,0:T(8,128)S(1)} %get-tuple-element.28), kind=kOutput, calls=%fused_computation.35 | convolution fusion | flops 805535744 | bytes 4194304 | tf_op jit(solution)/shard_map/mkb,bj->mkj/dot_general | solution.py:41
  105.1 3.6 %fusion.12 = f32[128,32,128]{2,0,1:T(8,128)S(1)} fusion(f32[128,32,128]{2,1,0:T(8,128)S(1)} %get-tuple-element.15), kind=kOutput, calls=%fused_computation.27 | convolution fusion | flops 805535744 | bytes 4194304 | tf_op jit(solution)/shard_map/mkb,bj->mkj/dot_general | solution.py:41
  108.7 3.6 %fusion.14 = f32[128,32,128]{2,0,1:T(8,128)S(1)} fusion(f32[128,32,128]{2,1,0:T(8,128)S(1)} %get-tuple-element.15), kind=kOutput, calls=%fused_computation.29 | convolution fusion | flops 805535744 | bytes 4194304 | tf_op jit(solution)/shard_map/mkb,bj->mkj/dot_general | solution.py:38
  112.3 4.0 %fusion.36 = f32[128,32,128]{2,0,1:T(8,128)S(1)} fusion(f32[128,32,128]{2,0,1:T(8,128)S(1)} %fusion.30, f32[128,32,128]{2,1,0:T(8,128)S(1)} %get-tuple-element.31), kind=kOutput, calls=%fused_computation.51 | convolution fusion | flops 806060032 | bytes 6291456 | tf_op jit(solution)/shard_map/mkb,bj->mkj/dot_general | solution.py:38
  116.3 3.7 %fusion.39 = f32[128,32,128]{2,0,1:T(8,128)S(1)} fusion(f32[128,32,128]{2,0,1:T(8,128)S(1)} %fusion.28, f32[128,32,128]{2,1,0:T(8,128)S(1)} %get-tuple-element.31), kind=kOutput, calls=%fused_computation.52 | convolution fusion | flops 806060032 | bytes 6291456 | tf_op jit(solution)/shard_map/mkb,bj->mkj/dot_general | solution.py:41
  120.0 3.6 %fusion.42 = f32[128,32,128]{2,0,1:T(8,128)S(1)} fusion(f32[128,32,128]{2,0,1:T(8,128)S(1)} %fusion.22, f32[128,32,128]{2,1,0:T(8,128)S(1)} %get-tuple-element.29), kind=kOutput, calls=%fused_computation.53 | convolution fusion | flops 806060032 | bytes 6291456 | tf_op jit(solution)/shard_map/mkb,bj->mkj/dot_general | solution.py:38
  123.6 3.8 %fusion.45 = f32[128,32,128]{2,0,1:T(8,128)S(1)} fusion(f32[128,32,128]{2,0,1:T(8,128)S(1)} %fusion.20, f32[128,32,128]{2,1,0:T(8,128)S(1)} %get-tuple-element.29), kind=kOutput, calls=%fused_computation.54 | convolution fusion | flops 806060032 | bytes 6291456 | tf_op jit(solution)/shard_map/mkb,bj->mkj/dot_general | solution.py:41
  127.4 3.7 %fusion.51 = f32[128,32,128]{2,0,1:T(8,128)S(1)} fusion(f32[128,32,128]{2,0,1:T(8,128)S(1)} %fusion.12, f32[128,32,128]{2,1,0:T(8,128)S(1)} %get-tuple-element.14), kind=kOutput, calls=%fused_computation.56 | convolution fusion | flops 806060032 | bytes 6291456 | tf_op jit(solution)/shard_map/mkb,bj->mkj/dot_general | solution.py:41
  131.1 4.5 %multiply_subtract_fusion.1 = (f32[128,32,128]{2,0,1:T(8,128)S(1)}, f32[128,32,128]{2,0,1:T(8,128)S(1)}, f32[128,32,128]{2,0,1:T(8,128)S(1)}, f32[128,32,128]{2,0,1:T(8,128)S(1)}) fusion(f32[128,32,128]{2,0,1:T(8,128)S(1)} %fusion.45, f32[128,32,128]{2,0,1:T(8,128)S(1)} %fusion.51, f32[128,32,128]{2,0,1:T(8,128)S(1)} %fusion.42, ...), kind=kOutput, calls=%fused_computation.15 | convolution fusion | flops 812351488 | bytes 23068672 | tf_op jit(solution)/shard_map/mkb,bj->mkj/dot_general | solution.py:38
  151.0 4.4 %multiply_subtract_fusion = (f32[128,32,128]{2,0,1:T(8,128)S(1)}, f32[128,32,128]{2,0,1:T(8,128)}, f32[128,32,128]{2,0,1:T(8,128)S(1)}, f32[128,32,128]{2,0,1:T(8,128)S(1)}) fusion(f32[128,32,128]{2,0,1:T(8,128)S(1)} %convolution_subtract_fusion, f32[32,128]{1,0:T(8,128)S(1)} %get-tuple-element.32, f32[32,128]{1,0:T(8,128)S(1)} %get-tuple-element.33, ...), kind=kOutput, calls=%fused_computation.14 | convolution fusion | flops 812351488 | bytes 18907136 | tf_op jit(solution)/shard_map/mkj,jb->mkb/dot_general | solution.py:54
  161.4 3.5 %all-to-all-start.1 = ((f32[1,128,2048]{1,0,2:T(1,128)}), f32[1,128,2048]{1,0,2:T(1,128)S(1)}, u32[]{:S(2)}, u32[]{:S(2)}) async-start(f32[1,128,2048]{1,0,2:T(1,128)} %bitcast.152), calls=%async_computation.1 | async-start | bytes 2097152 | tf_op jit(solution)/shard_map/all_to_all | solution.py:70
  167.4 10.6 %all-to-all-done.1 = f32[1,128,2048]{1,0,2:T(1,128)S(1)} async-done(((f32[1,128,2048]{1,0,2:T(1,128)}), f32[1,128,2048]{1,0,2:T(1,128)S(1)}, u32[]{:S(2)}, u32[]{:S(2)}) %all-to-all-start.1) | async-done | bytes 1048608 | tf_op jit(solution)/shard_map/all_to_all | solution.py:70
  182.1 5.1 %fusion = f32[512,2048]{1,0:T(8,128)} fusion(bf16[512,512]{1,0:T(8,128)(2,1)} %bitcast.155, bf16[1,2048,512]{2,1,0:T(8,128)(2,1)} %all-gather.2.cloned.1.call-done), kind=kOutput, calls=%fused_computation | convolution fusion | flops 1073741824 | bytes 6815744 | tf_op jit(solution)/shard_map/dot_general | solution.py:92
  187.2 3.8 %fusion.4 = f32[16,128,128]{2,0,1:T(8,128)S(1)} fusion(f32[128,32,128]{2,0,1:T(8,128)} %get-tuple-element.13), kind=kOutput, calls=%fused_computation.4 | convolution fusion | flops 100670464 | bytes 3145728 | tf_op jit(solution)/shard_map/mkb,ak->mab/dot_general | solution.py:59
  191.0 3.3 %fusion.69 = f32[128,16,128]{2,1,0:T(8,128)} fusion(f32[16,128,128]{2,0,1:T(8,128)S(1)} %fusion.4, f32[128,32,128]{2,0,1:T(8,128)S(1)} %get-tuple-element.12), kind=kOutput, calls=%fused_computation.66 | convolution fusion | flops 101194752 | bytes 4194304 | tf_op jit(solution)/shard_map/mkb,ak->mab/dot_general | solution.py:59
  196.9 3.5 %all-to-all-start.3 = ((f32[1,128,2048]{1,0,2:T(1,128)}), f32[1,128,2048]{1,0,2:T(1,128)S(1)}, u32[]{:S(2)}, u32[]{:S(2)}) async-start(f32[1,128,2048]{1,0,2:T(1,128)} %bitcast.24), calls=%async_computation.3 | async-start | bytes 2097152 | tf_op jit(solution)/shard_map/all_to_all | solution.py:70
  200.7 20.2 %all-to-all-done.3 = f32[1,128,2048]{1,0,2:T(1,128)S(1)} async-done(((f32[1,128,2048]{1,0,2:T(1,128)}), f32[1,128,2048]{1,0,2:T(1,128)S(1)}, u32[]{:S(2)}, u32[]{:S(2)}) %all-to-all-start.3) | async-done | bytes 1048608 | tf_op jit(solution)/shard_map/all_to_all | solution.py:70
  221.7 2.8 fusion.73
  227.3 49.4 %all-reduce.2.cloned.1.call-done = f32[512,2048]{1,0:T(8,128)} async-done(((f32[512,2048]{1,0:T(8,128)}), f32[512,2048]{1,0:T(8,128)}) %all-reduce.2.cloned.1.call-update) | async-done | bytes 4194320 | tf_op jit(solution)/shard_map/psum | solution.py:97
  276.7 4.9 %broadcast_multiply_fusion = f32[512,2048]{1,0:T(8,128)} fusion(f32[512,2048]{1,0:T(8,128)} %all-reduce.2.cloned.1.call-done), kind=kLoop, calls=%fused_computation.12 | loop fusion | flops 1048576 | bytes 8388608 | tf_op jit(solution)/shard_map/mul | solution.py:98
  (51 shorter events, 48.3 us)
Async XLA Ops:
  7.2 51.1 %copy-start = (bf16[512,2048]{1,0:T(8,128)(2,1)S(1)}, bf16[512,2048]{1,0:T(8,128)(2,1)}, u32[]{:S(2)}) copy-start(bf16[512,2048]{1,0:T(8,128)(2,1)} %param.10) | copy-start | bytes 6291460
  7.2 51.1 %all-gather.2.cloned.1.call-start = ((), (), s32[]{:S(2)}) async-start(), calls=%async_computation.4 | async-start | bytes 2621440 | tf_op jit(solution)/shard_map/all_gather | solution.py:90
  11.2 53.3 %all-to-all-start = ((f32[1,512,512]{2,0,1:T(1,128)}), f32[1,512,512]{2,0,1:T(1,128)}, u32[]{:S(2)}, u32[]{:S(2)}) async-start(f32[1,512,512]{2,0,1:T(1,128)} %fusion.76), calls=%async_computation | async-start | bytes 2097152 | tf_op jit(solution)/shard_map/all_to_all | solution.py:66
  58.3 3.9 %copy-start.7 = (bf16[1,512,512]{2,1,0:T(8,128)(2,1)S(1)}, bf16[1,512,512]{2,1,0:T(8,128)(2,1)}, u32[]{:S(2)}) copy-start(bf16[1,512,512]{2,1,0:T(8,128)(2,1)} %param.6) | copy-start | bytes 1572868
  61.2 1.0 copy-start.5
  64.4 17.4 %all-to-all-start.2 = ((f32[1,512,512]{2,0,1:T(1,128)}), f32[1,512,512]{2,0,1:T(1,128)S(1)}, u32[]{:S(2)}, u32[]{:S(2)}) async-start(f32[1,512,512]{2,0,1:T(1,128)} %copy.89), calls=%async_computation.2 | async-start | bytes 2097152 | tf_op jit(solution)/shard_map/all_to_all | solution.py:66
  82.9 3.9 %copy-start.3 = (f32[32,128,128]{2,0,1:T(8,128)S(1)}, f32[32,128,128]{2,0,1:T(8,128)}, u32[]{:S(2)}) copy-start(f32[32,128,128]{2,0,1:T(8,128)} %fusion.150) | copy-start | bytes 6291460
  83.0 3.9 %copy-start.4 = (f32[32,128,128]{2,0,1:T(8,128)S(1)}, f32[32,128,128]{2,0,1:T(8,128)}, u32[]{:S(2)}) copy-start(f32[32,128,128]{2,0,1:T(8,128)} %fusion.144) | copy-start | bytes 6291460
  84.9 1.9 copy-start.2
  161.4 16.6 %all-to-all-start.1 = ((f32[1,128,2048]{1,0,2:T(1,128)}), f32[1,128,2048]{1,0,2:T(1,128)S(1)}, u32[]{:S(2)}, u32[]{:S(2)}) async-start(f32[1,128,2048]{1,0,2:T(1,128)} %bitcast.152), calls=%async_computation.1 | async-start | bytes 2097152 | tf_op jit(solution)/shard_map/all_to_all | solution.py:70
  164.9 111.8 %all-reduce.2.cloned.1.call-start = ((), (), s32[]{:S(2)}) async-start(), calls=%async_computation.5 | async-start | bytes 8388608 | tf_op jit(solution)/shard_map/psum | solution.py:97
  196.9 24.1 %all-to-all-start.3 = ((f32[1,128,2048]{1,0,2:T(1,128)}), f32[1,128,2048]{1,0,2:T(1,128)S(1)}, u32[]{:S(2)}, u32[]{:S(2)}) async-start(f32[1,128,2048]{1,0,2:T(1,128)} %bitcast.24), calls=%async_computation.3 | async-start | bytes 2097152 | tf_op jit(solution)/shard_map/all_to_all | solution.py:70
  224.5 1.8 copy-start.6
  276.7 4.9 %copy-start.1 = (bf16[512,2048]{1,0:T(8,128)(2,1)S(1)}, bf16[512,2048]{1,0:T(8,128)(2,1)}, u32[]{:S(2)}) copy-start(bf16[512,2048]{1,0:T(8,128)(2,1)} %param.10) | copy-start | bytes 6291460
Sparse Core Ops, SparseCore 0:
  9.6 48.6 all-gather.1
  187.3 89.3 all-reduce.1
where the time goes:
time: 293 us; the launch traced here: 289 us
  waiting for transfers between devices  123 us (42%)
  matrix products  101 us (34%)
  local copies, waits for them, and re-layouts  19.1 us (7%)
  starting transfers between devices  16.6 us (6%)
  between operations  14.6 us (5%)
  other arithmetic  14.3 us (5%)
    psum x1, waiting for transfers between devices, shards(): weight_total = lax.psum(weight_part, ('dp', 'seq'))  49.4 us
    all_gather x1, waiting for transfers between devices, shards(): piece_rows = lax.all_gather(grad_out, 'chan', axis=1, tiled=True)[0]  40.5 us
    all_to_all x2, waiting for transfers between devices, to_blocks(): lax.all_to_all(whole_rows, 'seq', split_axis=2, concat_axis=1, tiled=True)  30.8 us
    dot_general x3, matrix products, forward_spectrum(): jnp.einsum('mkb,bj->mkj', real_mid, cos_second, precision=precise)  12.1 us
    dot_general x3, matrix products, forward_spectrum(): jnp.einsum('mkb,bj->mkj', real_mid, sin_second, precision=precise)  11.2 us
    dot_general x3, matrix products, forward_spectrum(): jnp.einsum('mkb,bj->mkj', imag_mid, sin_second, precision=precise)  11 us
    dot_general x3, matrix products, forward_spectrum(): jnp.einsum('mkb,bj->mkj', imag_mid, cos_second, precision=precise)  10.7 us
    all_to_all x2, starting transfers between devices, to_full(): lax.all_to_all(block_rows, 'seq', split_axis=1, concat_axis=2, tiled=True)  9.31 us
  transfers between devices with their start and end apart: 6, of which 5 were waited for; matrix products, arithmetic and copies ran while one was open for 14% of the time, Pallas kernels for 0%

commit v1 on v0

v1 whole, which is shorter than its diff:
```python
import functools
import math

import jax
import jax.numpy as jnp
import numpy as np
from jax import lax
from jax.experimental import pallas as pl
from jax.experimental.pallas import tpu as pltpu
from jax.sharding import PartitionSpec as P

LANES = 128
MESH = pl.DeviceIdType.MESH
VMEM_LIMIT = 56 * 1024 * 1024


def split_table(table):
    high = table.astype(jnp.bfloat16)
    low = (table - high.astype(np.float64)).astype(jnp.bfloat16)
    return [high, low]


def make_tables(slabs):
    total = 2 * slabs * LANES
    lane = np.arange(LANES, dtype=np.float64)
    turn = 2.0 * np.pi / LANES * (np.outer(lane, lane) % LANES)
    cos_lane, sin_lane = np.cos(turn), np.sin(turn)
    ahead = np.block([[cos_lane, -sin_lane], [sin_lane, cos_lane]])
    back = np.block([[cos_lane, sin_lane], [-sin_lane, cos_lane]]) / total
    twist = 2.0 * np.pi / total * np.outer(np.arange(slabs + 1, dtype=np.float64), lane)
    wide = lambda rows: np.broadcast_to(rows[:, None, :], (slabs + 1, 8, LANES)).astype(np.float32)
    return split_table(ahead) + split_table(back) + [wide(np.cos(twist)), wide(np.sin(twist))]


def add(left, right):
    if left is None:
        return right
    if right is None:
        return left
    return left + right


def sub(left, right):
    if right is None:
        return left
    if left is None:
        return -right
    return left - right


def mul(value, factor):
    return None if value is None else value * factor


def half_fft(size, points):
    if size == 2:
        return [(points[0], None), (points[0], None)]
    even, odd = half_fft(size // 2, points[::2]), half_fft(size // 2, points[1::2])
    bins = [None] * (size // 2 + 1)
    for k in range(size // 4 + 1):
        (e_re, e_im), (o_re, o_im) = even[k], odd[k]
        if k == 0:
            t_re, t_im = o_re, None
        elif k == size // 4:
            t_re, t_im = None, -o_re
        else:
            cos, sin = math.cos(2 * math.pi * k / size), math.sin(2 * math.pi * k / size)
            t_re = add(mul(o_re, cos), mul(o_im, sin))
            t_im = sub(mul(o_im, cos), mul(o_re, sin))
        if k != size // 4:
            bins[size // 2 - k] = (sub(e_re, t_re), sub(t_im, e_im))
        bins[k] = (add(e_re, t_re), add(e_im, t_im))
    return bins


def half_inverse(size, bins):
    if size == 2:
        return [bins[0][0] + bins[1][0]]
    even, odd = [], []
    for k in range(size // 4 + 1):
        (u_re, u_im), (v_re, v_im) = bins[k], bins[size // 2 - k]
        if k == 0:
            even.append((u_re + v_re, None))
            odd.append((u_re - v_re, None))
        elif k == size // 4:
            even.append((u_re + u_re, None))
            odd.append((-(u_im + u_im), None))
        else:
            cos, sin = math.cos(2 * math.pi * k / size), math.sin(2 * math.pi * k / size)
            d_re, d_im = u_re - v_re, add(u_im, v_im)
            even.append((u_re + v_re, sub(u_im, v_im)))
            odd.append((sub(d_re * cos, mul(d_im, sin)), add(d_re * sin, mul(d_im, cos))))
    points = [None] * (size // 2)
    points[::2], points[1::2] = half_inverse(size // 2, even), half_inverse(size // 2, odd)
    return points


def pass_rows(rows):
    return max(d for d in range(8, 577, 8) if rows % d == 0)


def three_dot(wide, high, low):
    big = wide.astype(jnp.bfloat16)
    small = (wide - big.astype(jnp.float32)).astype(jnp.bfloat16)
    dot = functools.partial(jnp.dot, preferred_element_type=jnp.float32)
    return dot(big, high) + (dot(small, high) + dot(big, low))


def slab_pass(load, spec, cos_ref, sin_ref, slabs, width):
    @pl.loop(0, width // 8)
    def _(step):
        row = pl.multiple_of(step * 8, 8)
        bins = half_fft(2 * slabs, [load(a, row) for a in range(slabs)])
        for k, (re, im) in enumerate(bins):
            cos, sin = cos_ref[k], sin_ref[k]
            rows = pl.ds(pl.multiple_of(k * width + row, 8), 8)
            spec[rows, :LANES] = add(re * cos, mul(im, sin))
            spec[rows, LANES:] = sub(mul(im, cos), re * sin)


def lane_pass(spec, out, ahead):
    rows = pass_rows(spec.shape[0])

    @pl.loop(0, spec.shape[0] // rows)
    def _(step):
        part = pl.ds(pl.multiple_of(step * rows, 8), rows)
        out[part, :] = three_dot(spec[part, :], ahead[0][...], ahead[1][...])


def filter_pass(spec, filt, ahead, back, conjugate):
    rows = pass_rows(spec.shape[0])

    @pl.loop(0, spec.shape[0] // rows)
    def _(step):
        part = pl.ds(pl.multiple_of(step * rows, 8), rows)
        signal = three_dot(spec[part, :], ahead[0][...], ahead[1][...])
        s_re, s_im = signal[:, :LANES], signal[:, LANES:]
        f_re, f_im = filt[part, :LANES], filt[part, LANES:]
        if conjugate:
            p_re, p_im = s_re * f_re + s_im * f_im, s_im * f_re - s_re * f_im
        else:
            p_re, p_im = s_re * f_re - s_im * f_im, s_im * f_re + s_re * f_im
        product = jnp.concatenate([p_re, p_im], axis=1)
        spec[part, :] = three_dot(product, back[0][...], back[1][...])


def slab_inverse(spec, full, cos_ref, sin_ref, slabs, width):
    @pl.loop(0, width // 8)
    def _(step):
        row = pl.multiple_of(step * 8, 8)
        bins = []
        for k in range(slabs + 1):
            rows = pl.ds(pl.multiple_of(k * width + row, 8), 8)
            re, im = spec[rows, :LANES], spec[rows, LANES:]
            cos, sin = cos_ref[k], sin_ref[k]
            bins.append((re * cos - im * sin, re * sin + im * cos))
        for a, point in enumerate(half_inverse(2 * slabs, bins)):
            full[a, pl.ds(row, 8), :] = point


def push(src, dst, sems, slot, device):
    copy = pltpu.make_async_remote_copy(
        src_ref=src, dst_ref=dst, send_sem=sems.at[0, slot], recv_sem=sems.at[1, slot],
        device_id=device, device_id_type=MESH,
    )
    copy.start()
    return copy


def greet(devices):
    barrier = pltpu.get_barrier_semaphore()
    for device in devices:
        pl.semaphore_signal(barrier, inc=1, device_id=device, device_id_type=MESH)
    pl.semaphore_wait(barrier, len(devices))


def forward_kernel(n, key_ref, value_ref, filt_ref, ah, al, bh, bl, cos_ref, sin_ref,
                   conv, fspec, mixed, full, spec, out_sems, back_sems):
    me = lax.axis_index("seq")
    local, channels = mixed.shape[0], mixed.shape[1]
    width, slabs = channels // n, local * n
    peers = [lax.rem(me + r, n) for r in range(1, n)]
    greet([{"seq": p} for p in peers])

    def slab_ids(p):
        return pl.ds(p * local, local)

    def channel_ids(p):
        return pl.ds(pl.multiple_of(p * width, width), width)

    waits = []
    for slot, p in enumerate(peers + [me]):
        rows = channel_ids(p)
        product = key_ref[rows, :].astype(jnp.float32) * value_ref[rows, :].astype(jnp.float32)
        for l in range(local):
            piece = product[:, l * LANES:(l + 1) * LANES]
            if slot < n - 1:
                mixed[l, rows, :] = piece
            else:
                full[me * local + l] = piece
        if slot < n - 1:
            waits.append(push(mixed.at[:, rows, :], full.at[slab_ids(me)], out_sems, slot, {"seq": p}))
    slab_pass(lambda a, row: filt_ref[pl.ds(row, 8), a * LANES:(a + 1) * LANES], spec, cos_ref, sin_ref, slabs, width)
    lane_pass(spec, fspec, (ah, al))
    for copy in waits:
        copy.wait()
    slab_pass(lambda a, row: full[a, pl.ds(row, 8), :], spec, cos_ref, sin_ref, slabs, width)
    filter_pass(spec, fspec, (ah, al), (bh, bl), False)
    slab_inverse(spec, full, cos_ref, sin_ref, slabs, width)
    waits = []
    for slot, p in enumerate(peers):
        waits.append(push(full.at[slab_ids(p)], conv.at[:, channel_ids(me), :], back_sems, slot, {"seq": p}))
    for l in range(local):
        conv[l, channel_ids(me), :] = full[me * local + l]
    for copy in waits:
        copy.wait()


def backward_kernel(n, scale, query_ref, key_ref, value_ref, weight_ref, grad_ref, conv, fspec,
                    ah, al, bh, bl, cos_ref, sin_ref,
                    grad_query, grad_key, grad_value, grad_weight,
                    gate, full, back, turned, spec, gated, pair_send, pair_recv, own_part, ring_send, ring_recv,
                    out_sems, back_sems, pair_sems, ring_sems, share_sems, final_sems):
    me, core = lax.axis_index("seq"), lax.axis_index("dp")
    local, channels = gate.shape[0], gate.shape[1]
    width, slabs = channels // n, local * n
    half, cols = channels // 2, grad_weight.shape[1] // n
    peers = [lax.rem(me + r, n) for r in range(1, n)]
    other = {"dp": 1 - core}
    greet([{"seq": p} for p in peers] + [other])

    def slab_ids(p):
        return pl.ds(p * local, local)

    def channel_ids(p):
        return pl.ds(pl.multiple_of(p * width, width), width)

    waits = []
    for slot, p in enumerate(peers + [me]):
        rows = channel_ids(p)
        mid = jnp.dot(weight_ref[rows, :], grad_ref[...], preferred_element_type=jnp.float32)
        query = query_ref[rows, :].astype(jnp.float32)
        for l in range(local):
            lanes = slice(l * LANES, (l + 1) * LANES)
            mid_l, query_l, conv_l = mid[:, lanes], query[:, lanes], conv[l, rows, :]
            if slot < n - 1:
                gate[l, rows, :] = query_l * mid_l
            else:
                full[me * local + l] = query_l * mid_l
            grad_query[rows, lanes] = (mid_l * conv_l).astype(jnp.bfloat16)
            gated[rows, lanes] = (query_l * conv_l).astype(jnp.bfloat16)
        if slot < n - 1:
            waits.append(push(gate.at[:, rows, :], full.at[slab_ids(me)], out_sems, slot, {"seq": p}))

    def weight_half(which, dest):
        rows = pl.ds(pl.multiple_of(which * half, half), half)

        @pl.loop(0, n)
        def _(step):
            dest[step] = lax.dot_general(
                gated[rows, :], grad_ref[pl.ds(pl.multiple_of(step * cols, cols), cols), :],
                (((1,), (1,)), ((), ())), preferred_element_type=jnp.float32,
            )

    weight_half(1 - core, pair_send)
    pair = push(pair_send, pair_recv, pair_sems, 0, other)
    weight_half(core, own_part)
    pair.wait()
    ring = []
    for slot, p in enumerate(peers):
        ring_send[slot] = (own_part[p] + pair_recv[p]).astype(jnp.bfloat16)
        ring.append(push(ring_send.at[slot], ring_recv.at[slot], ring_sems, slot, {"seq": p}))

    for copy in waits:
        copy.wait()
    slab_pass(lambda a, row: full[a, pl.ds(row, 8), :], spec, cos_ref, sin_ref, slabs, width)
    filter_pass(spec, fspec, (ah, al), (bh, bl), True)
    slab_inverse(spec, back, cos_ref, sin_ref, slabs, width)
    waits = []
    for slot, p in enumerate(peers):
        waits.append(push(back.at[slab_ids(p)], turned.at[:, channel_ids(me), :], back_sems, slot, {"seq": p}))
    for l in range(local):
        turned[l, channel_ids(me), :] = back[me * local + l]

    total = own_part[me] + pair_recv[me]
    for slot, copy in enumerate(ring):
        copy.wait()
        total = total + ring_recv[slot].astype(jnp.float32)
    mine = pl.ds(pl.multiple_of(core * half, half), half)

    def chunk(p):
        return grad_weight.at[mine, pl.ds(pl.multiple_of(p * cols, cols), cols)]

    chunk(me)[...] = (total * scale).astype(jnp.bfloat16)
    share = [push(chunk(me), chunk(me), share_sems, slot, {"seq": p}) for slot, p in enumerate(peers)]
    final = [push(chunk(me), chunk(me), final_sems, n - 1, other)]

    for copy in waits:
        copy.wait()
    for l in range(local):
        lanes = slice(l * LANES, (l + 1) * LANES)
        mixed = turned[l]
        grad_key[:, lanes] = (mixed * value_ref[:, lanes].astype(jnp.float32)).astype(jnp.bfloat16)
        grad_value[:, lanes] = (mixed * key_ref[:, lanes].astype(jnp.float32)).astype(jnp.bfloat16)
    for slot, copy in enumerate(share):
        copy.wait()
        source = lax.rem(me + n - slot - 1, n)
        final.append(push(chunk(source), chunk(source), final_sems, slot, other))
    for copy in final:
        copy.wait()


def sems(count):
    return pltpu.SemaphoreType.DMA((2, count))


def shards(query_proj, key_proj, value_proj, grad_out, out_weight, long_filter):
    n = lax.axis_size("seq")
    channels, positions = query_proj.shape[1:]
    local = positions // LANES
    slabs, width = local * n, channels // n
    spec_rows = (slabs + 1) * width
    features = out_weight.shape[1]
    tables = [jnp.asarray(t) for t in make_tables(slabs)]
    vmem = pl.BlockSpec(memory_space=pltpu.VMEM)
    f32, bf16 = jnp.float32, jnp.bfloat16

    pieces = lax.all_gather(grad_out[0], "chan", axis=0, tiled=True)
    fft_flops = 12 * spec_rows * 256 * 256
    conv, fspec = pl.pallas_call(
        functools.partial(forward_kernel, n),
        out_shape=(
            jax.ShapeDtypeStruct((local, channels, LANES), f32),
            jax.ShapeDtypeStruct((spec_rows, 2 * LANES), f32),
        ),
        in_specs=[vmem] * 9,
        out_specs=(vmem, vmem),
        scratch_shapes=[
            pltpu.VMEM((local, channels, LANES), f32),
            pltpu.VMEM((slabs, width, LANES), f32),
            pltpu.VMEM((spec_rows, 2 * LANES), f32),
            sems(n - 1), sems(n - 1),
        ],
        compiler_params=pltpu.CompilerParams(
            collective_id=0, has_side_effects=True, vmem_limit_bytes=VMEM_LIMIT
        ),
        cost_estimate=pl.CostEstimate(flops=20 * fft_flops, bytes_accessed=64 * channels * positions, transcendentals=0),
        name="forward",
    )(key_proj[0], value_proj[0], long_filter, *tables)

    scale = 1.0 / math.sqrt(lax.axis_size("dp") * long_filter.shape[1])
    half, cols = channels // 2, features // n
    block = jax.ShapeDtypeStruct((channels, positions), bf16)
    grad_query, grad_key, grad_value, grad_weight = pl.pallas_call(
        functools.partial(backward_kernel, n, scale),
        out_shape=(block, block, block, jax.ShapeDtypeStruct((channels, features), bf16)),
        in_specs=[vmem] * 13,
        out_specs=(vmem,) * 4,
        scratch_shapes=[
            pltpu.VMEM((local, channels, LANES), f32),
            pltpu.VMEM((slabs, width, LANES), f32),
            pltpu.VMEM((slabs, width, LANES), f32),
            pltpu.VMEM((local, channels, LANES), f32),
            pltpu.VMEM((spec_rows, 2 * LANES), f32),
            pltpu.VMEM((channels, positions), bf16),
            pltpu.VMEM((n, half, cols), f32),
            pltpu.VMEM((n, half, cols), f32),
            pltpu.VMEM((n, half, cols), f32),
            pltpu.VMEM((n - 1, half, cols), bf16),
            pltpu.VMEM((n - 1, half, cols), bf16),
            sems(n - 1), sems(n - 1), sems(1), sems(n - 1), sems(n - 1), sems(n),
        ],
        compiler_params=pltpu.CompilerParams(
            collective_id=1, has_side_effects=True, vmem_limit_bytes=VMEM_LIMIT
        ),
        cost_estimate=pl.CostEstimate(flops=20 * fft_flops, bytes_accessed=64 * channels * positions, transcendentals=0),
        name="backward",
    )(query_proj[0], key_proj[0], value_proj[0], out_weight, pieces, conv, fspec, *tables)
    return (grad_query[None], grad_key[None], grad_value[None], grad_weight.astype(f32))


def solution(mesh):
    placed = (
        P("dp", "chan", "seq"),
        P("dp", "chan", "seq"),
        P("dp", "chan", "seq"),
        P("dp", "chan", "seq"),
        P("chan", None),
        P(("chan", "seq"), None),
    )
    return jax.shard_map(
        shards,
        mesh=mesh,
        in_specs=placed,
        out_specs=(
            P("dp", "chan", "seq"),
            P("dp", "chan", "seq"),
            P("dp", "chan", "seq"),
            P("chan", None),
        ),
        check_vma=False,
    )
```

time: 293 us -> 128 us (0.44); the launches traced: 289 us -> 128 us
  waiting for transfers between devices: 123 us -> 12.2 us
  matrix products: 101 us -> 0 us
  Pallas kernels: 0 us -> 95.4 us
  local copies, waits for them, and re-layouts: 19.1 us -> 2.39 us
  starting transfers between devices: 16.6 us -> 0.04 us
  other arithmetic: 14.3 us -> 4.22 us
    dot_general x32 -> x0, matrix products: 101 us -> none  [the longest x3 12.1 us: forward_spectrum(): jnp.einsum('mkb,bj->mkj', real_mid, cos_second, precision=precise)]
    pallas_call x0 -> x2, Pallas kernels: none -> 95.4 us  [the longest x1 56.6 us: shards(): pl.pallas_call(functools.partial(backward_kernel, n, scale), out_shape=(b...]
    psum x1 -> x0, waiting for transfers between devices: 49.4 us -> none  [shards(): weight_total = lax.psum(weight_part, ('dp', 'seq'))]
    all_to_all x4 -> x0, waiting for transfers between devices: 32 us -> none  [the longest x2 30.8 us: to_blocks(): lax.all_to_all(whole_rows, 'seq', split_axis=2, concat_axis=1, tiled=True)]
    all_gather x1, waiting for transfers between devices: 40.5 us -> 11.6 us  [shards(): pieces = lax.all_gather(grad_out[0], 'chan', axis=0, tiled=True)]
    all_to_all x4 -> x0, starting transfers between devices: 16.3 us -> none  [the longest x2 9.31 us: to_full(): lax.all_to_all(block_rows, 'seq', split_axis=1, concat_axis=2, tiled=True)]
    mul x2 -> x0, other arithmetic: 8.19 us -> none  [the longest x1 4.94 us: shards(): grad_weight = weight_total * (1.0 / math.sqrt(lax.axis_size('dp') * length))]
    convert_element_type x2 -> x0, local copies, waits for them, and re-layouts: 4.28 us -> none  [the longest x1 2.24 us: shards(): query_vals = query_proj[0].astype(jnp.float32)]
  transfers between devices with their start and end apart: 6 -> 1, of which waited for: 5 -> 1; matrix products, arithmetic and copies ran while one was open for 14% -> 0% of each run, Pallas kernels for 0% -> 30%
where the time goes in v1:
time: 128 us
  Pallas kernels  95.4 us (75%)
  between operations  14.1 us (11%)
  waiting for transfers between devices  12.2 us (10%)
  other arithmetic  4.22 us (3%)
  local copies, waits for them, and re-layouts  2.39 us (2%)
    pallas_call x1, Pallas kernels, shards(): pl.pallas_call(functools.partial(backward_kernel, n, scale), out_shape=(b...  56.6 us
    pallas_call x1, Pallas kernels, shards(): pl.pallas_call(functools.partial(forward_kernel, n), out_shape=(jax.Shape...  38.8 us
    all_gather x1, waiting for transfers between devices, shards(): pieces = lax.all_gather(grad_out[0], 'chan', axis=0, tiled=True)  11.6 us
    convert_element_type x1, other arithmetic, shards(): grad_weight.astype(f32)  4.22 us
  transfers between devices with their start and end apart: 1, of which 1 were waited for; matrix products, arithmetic and copies ran while one was open for 0% of the time, Pallas kernels for 30%

profile of v1, /device:TPU:0, one launch (start us, length us, event | category | flops | bytes accessed | tf_op | source)
XLA Modules:
  0.0 128.3 jit_solution(13811801523185526955)
XLA Ops:
  7.2 0.0 all-gather.3.cloned.1.call-start
  7.2 0.7 all-gather.3.cloned.1.call-update
  7.9 38.8 %forward.1 = (f32[4,512,128]{2,1,0:T(8,128)}, f32[2176,256]{1,0:T(8,128)}) custom-call(bf16[512,512]{1,0:T(8,128)(2,1)} %bitcast.12, bf16[512,512]{1,0:T(8,128)(2,1)} %bitcast.14, f32[128,2048]{1,0:T(8,128)} %filt_ref.1, bf16[256,256]{1,0:T(8,128)(2,1)} %constant.12.clone.ah, bf16[256,256]{1,0:T(8,128)(2,1)} %constant.13.clone.al, ...), custom_call_target="tpu_custom_call" | custom-call | flops 34225520640 | bytes 16777216 | tf_op jit(solution)/shard_map/forward/pallas_call | solution.py:330
  46.7 11.6 %all-gather.3.cloned.1.call-done = bf16[1,2048,512]{2,1,0:T(8,128)(2,1)} async-done(((bf16[1,512,512]{2,1,0:T(8,128)(2,1)}), bf16[1,2048,512]{2,1,0:T(8,128)(2,1)}) %all-gather.3.cloned.1.call-update) | async-done | bytes 2097168 | tf_op jit(solution)/shard_map/all_gather | solution.py:328
  58.2 56.6 %backward.1 = (bf16[512,512]{1,0:T(8,128)(2,1)}, bf16[512,512]{1,0:T(8,128)(2,1)}, bf16[512,512]{1,0:T(8,128)(2,1)}, bf16[512,2048]{1,0:T(8,128)(2,1)}) custom-call(bf16[512,512]{1,0:T(8,128)(2,1)} %bitcast.11, bf16[512,512]{1,0:T(8,128)(2,1)} %bitcast.13, bf16[512,512]{1,0:T(8,128)(2,1)} %bitcast.15, bf16[512,2048]{1,0:T(8,128)(2,1)} %weight_ref.1, ...), custom_call_target="tpu_custom_call" | custom-call | flops 34225520640 | bytes 16777216 | tf_op jit(solution)/shard_map/backward/pallas_call | solution.py:354
  114.8 0.0 copy-start.2
  114.8 0.0 copy-start.1
  114.8 4.2 %convert_element_type.3 = f32[512,2048]{1,0:T(8,128)} convert(bf16[512,2048]{1,0:T(8,128)(2,1)} %get-tuple-element.15) | non-fusion elementwise | flops 1048576 | bytes 6291456 | tf_op jit(solution)/shard_map/convert_element_type | solution.py:379
  119.1 0.0 copy-done.2
  119.1 0.0 copy-start
  119.1 0.8 copy.19
  119.9 0.0 copy-done.1
  119.9 0.8 copy.20
  120.7 0.0 copy-done
  120.7 0.8 copy.21
Async XLA Ops:
  7.2 51.1 %all-gather.3.cloned.1.call-start = ((), (), s32[]{:S(2)}) async-start(), calls=%async_computation | async-start | bytes 2621440 | tf_op jit(solution)/shard_map/all_gather | solution.py:328
  114.8 4.2 %copy-start.2 = (bf16[512,512]{1,0:T(8,128)(2,1)S(1)}, bf16[512,512]{1,0:T(8,128)(2,1)}, u32[]{:S(2)}) copy-start(bf16[512,512]{1,0:T(8,128)(2,1)} %get-tuple-element.12) | copy-start | bytes 1572868
  114.8 5.0 %copy-start.1 = (bf16[512,512]{1,0:T(8,128)(2,1)S(1)}, bf16[512,512]{1,0:T(8,128)(2,1)}, u32[]{:S(2)}) copy-start(bf16[512,512]{1,0:T(8,128)(2,1)} %get-tuple-element.13) | copy-start | bytes 1572868
  119.1 1.6 %copy-start = (bf16[512,512]{1,0:T(8,128)(2,1)S(1)}, bf16[512,512]{1,0:T(8,128)(2,1)}, u32[]{:S(2)}) copy-start(bf16[512,512]{1,0:T(8,128)(2,1)} %get-tuple-element.14) | copy-start | bytes 1572868
Sparse Core Ops, SparseCore 0:
  9.6 48.6 all-gather.2

commit v2 on v1

--- a/solution.py
+++ b/solution.py
@@ -174,13 +174,23 @@
     pl.semaphore_wait(barrier, len(devices))
 
 
-def forward_kernel(n, key_ref, value_ref, filt_ref, ah, al, bh, bl, cos_ref, sin_ref,
-                   conv, fspec, mixed, full, spec, out_sems, back_sems):
-    me = lax.axis_index("seq")
+def kernel(n, nz, parts, scale, query_ref, key_ref, value_ref, own_ref, weight_ref, filt_ref,
+           ah, al, bh, bl, cos_ref, sin_ref,
+           grad_query, grad_key, grad_value, grad_weight,
+           pieces, mixed, full, conv, fspec, spec, gate, gate_full, turned, gated,
+           pair_send, pair_recv, own_part, ring_send, ring_recv,
+           mix_sems, conv_sems, gate_sems, back_sems, pair_sems, ring_sems, share_sems, final_sems, line_sems,
+           own_sem):
+    me, core, level = lax.axis_index("seq"), lax.axis_index("dp"), lax.axis_index("chan")
     local, channels = mixed.shape[0], mixed.shape[1]
     width, slabs = channels // n, local * n
+    part_width = width // parts
+    half, cols = channels // 2, grad_weight.shape[1] // n
+    piece = own_ref.shape[0]
     peers = [lax.rem(me + r, n) for r in range(1, n)]
-    greet([{"seq": p} for p in peers])
+    levels = [lax.rem(level + r, nz) for r in range(1, nz)]
+    other = {"dp": 1 - core}
+    greet([{"seq": p} for p in peers] + [other] + [{"chan": z} for z in levels])
 
     def slab_ids(p):
         return pl.ds(p * local, local)
@@ -188,69 +198,125 @@
     def channel_ids(p):
         return pl.ds(pl.multiple_of(p * width, width), width)
 
-    waits = []
-    for slot, p in enumerate(peers + [me]):
+    def part_ids(p, h):
+        return pl.ds(pl.multiple_of(p * width + h * part_width, part_width), part_width)
+
+    def piece_ids(z):
+        return pl.ds(pl.multiple_of(z * piece, piece), piece)
+
+    def line(side, distance, hop):
+        sign = 1 if side == 0 else -1
+        origin = level - sign * (distance - hop)
+        target = level + sign * hop
+        ok = (origin >= 0) & (origin < nz) & (target >= 0) & (target < nz)
+        source = own_ref if distance == hop else pieces.at[piece_ids(lax.rem(origin + nz, nz))]
+        copy = pltpu.make_async_remote_copy(
+            src_ref=source, dst_ref=pieces.at[piece_ids(lax.rem(origin + nz, nz))],
+            send_sem=line_sems.at[0, side, distance - 1], recv_sem=line_sems.at[1, side, distance - 1],
+            device_id={"chan": lax.rem(target + nz, nz)}, device_id_type=MESH,
+        )
+        return ok, copy
+
+    def line_start(side, distance, hop):
+        ok, copy = line(side, distance, hop)
+        pl.when(ok)(copy.start)
+
+    def line_sent(side, distance, hop):
+        ok, copy = line(side, distance, hop)
+        pl.when(ok)(copy.wait_send)
+
+    def line_arrived(side, distance):
+        origin = level - (1 if side == 0 else -1) * distance
+        rows = piece_ids(lax.rem(origin + nz, nz))
+        copy = pltpu.make_async_remote_copy(
+            src_ref=own_ref, dst_ref=pieces.at[rows],
+            send_sem=line_sems.at[0, side, distance - 1], recv_sem=line_sems.at[1, side, distance - 1],
+            device_id={"chan": lax.rem(origin + nz, nz)}, device_id_type=MESH,
+        )
+        pl.when((origin >= 0) & (origin < nz))(copy.wait_recv)
+
+    direct = min(2, nz - 1)
+    for distance in range(direct, 0, -1):
+        for side in range(2):
+            line_start(side, distance, distance)
+    keep = pltpu.make_async_copy(own_ref, pieces.at[piece_ids(level)], own_sem)
+    keep.start()
+
+    def leave(block, fulls, leg, h):
+        return [
+            push(block.at[:, part_ids(p, h), :], fulls.at[h, slab_ids(me)], leg, h * (n - 1) + slot, {"seq": p})
+            for slot, p in enumerate(peers)
+        ]
+
+    def come_home(fulls, block, leg, h):
+        copies = [
+            push(fulls.at[h, slab_ids(p)], block.at[:, part_ids(me, h), :], leg, h * (n - 1) + slot, {"seq": p})
+            for slot, p in enumerate(peers)
+        ]
+        for l in range(local):
+            block[l, part_ids(me, h), :] = fulls[h, me * local + l]
+        return copies
+
+    def own_slabs(block, fulls):
+        for h in range(parts):
+            for l in range(local):
+                fulls[h, me * local + l] = block[l, part_ids(me, h), :]
+
+    def convolve(fulls, h, conjugate):
+        slab_pass(lambda a, row: fulls[h, a, pl.ds(row, 8), :], spec, cos_ref, sin_ref, slabs, part_width)
+        filter_pass(spec, fspec.at[h], (ah, al), (bh, bl), conjugate)
+        slab_inverse(spec, fulls.at[h], cos_ref, sin_ref, slabs, part_width)
+
+    out = []
+    for p in peers + [me]:
         rows = channel_ids(p)
         product = key_ref[rows, :].astype(jnp.float32) * value_ref[rows, :].astype(jnp.float32)
         for l in range(local):
-            piece = product[:, l * LANES:(l + 1) * LANES]
-            if slot < n - 1:
-                mixed[l, rows, :] = piece
-            else:
-                full[me * local + l] = piece
-        if slot < n - 1:
-            waits.append(push(mixed.at[:, rows, :], full.at[slab_ids(me)], out_sems, slot, {"seq": p}))
-    slab_pass(lambda a, row: filt_ref[pl.ds(row, 8), a * LANES:(a + 1) * LANES], spec, cos_ref, sin_ref, slabs, width)
-    lane_pass(spec, fspec, (ah, al))
-    for copy in waits:
+            mixed[l, rows, :] = product[:, l * LANES:(l + 1) * LANES]
+    for h in range(parts):
+        out.append(leave(mixed, full, mix_sems, h))
+    own_slabs(mixed, full)
+    for h in range(parts):
+        slab_pass(
+            lambda a, row: filt_ref[pl.ds(pl.multiple_of(h * part_width + row, 8), 8), a * LANES:(a + 1) * LANES],
+            spec, cos_ref, sin_ref, slabs, part_width,
+        )
+        lane_pass(spec, fspec.at[h], (ah, al))
+    home = []
+    for h in range(parts):
+        for copy in out[h]:
+            copy.wait()
+        convolve(full, h, False)
+        home.extend(come_home(full, conv, conv_sems, h))
+    for distance in range(3, nz):
+        for side in range(2):
+            line_arrived(side, distance - 1)
+            line_start(side, distance, 1)
+    for copy in home:
         copy.wait()
-    slab_pass(lambda a, row: full[a, pl.ds(row, 8), :], spec, cos_ref, sin_ref, slabs, width)
-    filter_pass(spec, fspec, (ah, al), (bh, bl), False)
-    slab_inverse(spec, full, cos_ref, sin_ref, slabs, width)
-    waits = []
-    for slot, p in enumerate(peers):
-        waits.append(push(full.at[slab_ids(p)], conv.at[:, channel_ids(me), :], back_sems, slot, {"seq": p}))
-    for l in range(local):
-        conv[l, channel_ids(me), :] = full[me * local + l]
-    for copy in waits:
-        copy.wait()
-
-
-def backward_kernel(n, scale, query_ref, key_ref, value_ref, weight_ref, grad_ref, conv, fspec,
-                    ah, al, bh, bl, cos_ref, sin_ref,
-                    grad_query, grad_key, grad_value, grad_weight,
-                    gate, full, back, turned, spec, gated, pair_send, pair_recv, own_part, ring_send, ring_recv,
-                    out_sems, back_sems, pair_sems, ring_sems, share_sems, final_sems):
-    me, core = lax.axis_index("seq"), lax.axis_index("dp")
-    local, channels = gate.shape[0], gate.shape[1]
-    width, slabs = channels // n, local * n
-    half, cols = channels // 2, grad_weight.shape[1] // n
-    peers = [lax.rem(me + r, n) for r in range(1, n)]
-    other = {"dp": 1 - core}
-    greet([{"seq": p} for p in peers] + [other])
-
-    def slab_ids(p):
-        return pl.ds(p * local, local)
-
-    def channel_ids(p):
-        return pl.ds(pl.multiple_of(p * width, width), width)
-
-    waits = []
+    keep.wait()
+    for side in range(2):
+        for distance in range(1, nz):
+            if not 2 <= distance < nz - 1:
+                line_arrived(side, distance)
+            line_sent(side, distance, distance if distance <= direct else 1)
+
+    out = [[] for _ in range(parts)]
     for slot, p in enumerate(peers + [me]):
         rows = channel_ids(p)
-        mid = jnp.dot(weight_ref[rows, :], grad_ref[...], preferred_element_type=jnp.float32)
+        mid = jnp.dot(weight_ref[rows, :], pieces[...], preferred_element_type=jnp.float32)
         query = query_ref[rows, :].astype(jnp.float32)
         for l in range(local):
             lanes = slice(l * LANES, (l + 1) * LANES)
             mid_l, query_l, conv_l = mid[:, lanes], query[:, lanes], conv[l, rows, :]
-            if slot < n - 1:
-                gate[l, rows, :] = query_l * mid_l
-            else:
-                full[me * local + l] = query_l * mid_l
+            gate[l, rows, :] = query_l * mid_l
             grad_query[rows, lanes] = (mid_l * conv_l).astype(jnp.bfloat16)
             gated[rows, lanes] = (query_l * conv_l).astype(jnp.bfloat16)
         if slot < n - 1:
-            waits.append(push(gate.at[:, rows, :], full.at[slab_ids(me)], out_sems, slot, {"seq": p}))
+            out[0].append(push(gate.at[:, part_ids(p, 0), :], gate_full.at[0, slab_ids(me)], gate_sems, slot, {"seq": p}))
+    for h in range(1, parts):
+        out[h] = leave(gate, gate_full, gate_sems, h)
+    own_slabs(gate, gate_full)
 
     def weight_half(which, dest):
         rows = pl.ds(pl.multiple_of(which * half, half), half)
@@ -258,29 +324,25 @@
         @pl.loop(0, n)
         def _(step):
             dest[step] = lax.dot_general(
-                gated[rows, :], grad_ref[pl.ds(pl.multiple_of(step * cols, cols), cols), :],
+                gated[rows, :], pieces[pl.ds(pl.multiple_of(step * cols, cols), cols), :],
                 (((1,), (1,)), ((), ())), preferred_element_type=jnp.float32,
             )
 
     weight_half(1 - core, pair_send)
     pair = push(pair_send, pair_recv, pair_sems, 0, other)
     weight_half(core, own_part)
-    pair.wait()
-    ring = []
-    for slot, p in enumerate(peers):
-        ring_send[slot] = (own_part[p] + pair_recv[p]).astype(jnp.bfloat16)
-        ring.append(push(ring_send.at[slot], ring_recv.at[slot], ring_sems, slot, {"seq": p}))
-
-    for copy in waits:
-        copy.wait()
-    slab_pass(lambda a, row: full[a, pl.ds(row, 8), :], spec, cos_ref, sin_ref, slabs, width)
-    filter_pass(spec, fspec, (ah, al), (bh, bl), True)
-    slab_inverse(spec, back, cos_ref, sin_ref, slabs, width)
-    waits = []
-    for slot, p in enumerate(peers):
-        waits.append(push(back.at[slab_ids(p)], turned.at[:, channel_ids(me), :], back_sems, slot, {"seq": p}))
-    for l in range(local):
-        turned[l, channel_ids(me), :] = back[me * local + l]
+
+    home, ring = [], []
+    for h in range(parts):
+        for copy in out[h]:
+            copy.wait()
+        convolve(gate_full, h, True)
+        home.extend(come_home(gate_full, turned, back_sems, h))
+        if h == 0:
+            pair.wait()
+            for slot, p in enumerate(peers):
+                ring_send[slot] = (own_part[p] + pair_recv[p]).astype(jnp.bfloat16)
+                ring.append(push(ring_send.at[slot], ring_recv.at[slot], ring_sems, slot, {"seq": p}))
 
     total = own_part[me] + pair_recv[me]
     for slot, copy in enumerate(ring):
@@ -295,13 +357,13 @@
     share = [push(chunk(me), chunk(me), share_sems, slot, {"seq": p}) for slot, p in enumerate(peers)]
     final = [push(chunk(me), chunk(me), final_sems, n - 1, other)]
 
-    for copy in waits:
+    for copy in home:
         copy.wait()
     for l in range(local):
         lanes = slice(l * LANES, (l + 1) * LANES)
-        mixed = turned[l]
-        grad_key[:, lanes] = (mixed * value_ref[:, lanes].astype(jnp.float32)).astype(jnp.bfloat16)
-        grad_value[:, lanes] = (mixed * key_ref[:, lanes].astype(jnp.float32)).astype(jnp.bfloat16)
+        back = turned[l]
+        grad_key[:, lanes] = (back * value_ref[:, lanes].astype(jnp.float32)).astype(jnp.bfloat16)
+        grad_value[:, lanes] = (back * key_ref[:, lanes].astype(jnp.float32)).astype(jnp.bfloat16)
     for slot, copy in enumerate(share):
         copy.wait()
         source = lax.rem(me + n - slot - 1, n)
@@ -319,63 +381,50 @@
     channels, positions = query_proj.shape[1:]
     local = positions // LANES
     slabs, width = local * n, channels // n
-    spec_rows = (slabs + 1) * width
+    nz = lax.axis_size("chan")
+    parts = 2
+    part_width = width // parts
+    spec_rows = (slabs + 1) * part_width
     features = out_weight.shape[1]
     tables = [jnp.asarray(t) for t in make_tables(slabs)]
-    vmem = pl.BlockSpec(memory_space=pltpu.VMEM)
     f32, bf16 = jnp.float32, jnp.bfloat16
-
-    pieces = lax.all_gather(grad_out[0], "chan", axis=0, tiled=True)
-    fft_flops = 12 * spec_rows * 256 * 256
-    conv, fspec = pl.pallas_call(
-        functools.partial(forward_kernel, n),
-        out_shape=(
-            jax.ShapeDtypeStruct((local, channels, LANES), f32),
-            jax.ShapeDtypeStruct((spec_rows, 2 * LANES), f32),
-        ),
-        in_specs=[vmem] * 9,
-        out_specs=(vmem, vmem),
-        scratch_shapes=[
-            pltpu.VMEM((local, channels, LANES), f32),
-            pltpu.VMEM((slabs, width, LANES), f32),
-            pltpu.VMEM((spec_rows, 2 * LANES), f32),
-            sems(n - 1), sems(n - 1),
-        ],
-        compiler_params=pltpu.CompilerParams(
-            collective_id=0, has_side_effects=True, vmem_limit_bytes=VMEM_LIMIT
-        ),
-        cost_estimate=pl.CostEstimate(flops=20 * fft_flops, bytes_accessed=64 * channels * positions, transcendentals=0),
-        name="forward",
-    )(key_proj[0], value_proj[0], long_filter, *tables)
-
     scale = 1.0 / math.sqrt(lax.axis_size("dp") * long_filter.shape[1])
     half, cols = channels // 2, features // n
+    vmem = pl.BlockSpec(memory_space=pltpu.VMEM)
     block = jax.ShapeDtypeStruct((channels, positions), bf16)
+    rows = pltpu.VMEM((local, channels, LANES), f32)
+    whole = pltpu.VMEM((parts, slabs, part_width, LANES), f32)
     grad_query, grad_key, grad_value, grad_weight = pl.pallas_call(
-        functools.partial(backward_kernel, n, scale),
+        functools.partial(kernel, n, nz, parts, scale),
         out_shape=(block, block, block, jax.ShapeDtypeStruct((channels, features), bf16)),
-        in_specs=[vmem] * 13,
+        in_specs=[vmem] * 12,
         out_specs=(vmem,) * 4,
         scratch_shapes=[
-            pltpu.VMEM((local, channels, LANES), f32),
-            pltpu.VMEM((slabs, width, LANES), f32),
-            pltpu.VMEM((slabs, width, LANES), f32),
-            pltpu.VMEM((local, channels, LANES), f32),
+            pltpu.VMEM((features, positions), bf16),
+            rows, whole, rows,
+            pltpu.VMEM((parts, spec_rows, 2 * LANES), f32),
             pltpu.VMEM((spec_rows, 2 * LANES), f32),
+            rows, whole, rows,
             pltpu.VMEM((channels, positions), bf16),
             pltpu.VMEM((n, half, cols), f32),
             pltpu.VMEM((n, half, cols), f32),
             pltpu.VMEM((n, half, cols), f32),
             pltpu.VMEM((n - 1, half, cols), bf16),
             pltpu.VMEM((n - 1, half, cols), bf16),
-            sems(n - 1), sems(n - 1), sems(1), sems(n - 1), sems(n - 1), sems(n),
+            sems(parts * (n - 1)), sems(parts * (n - 1)), sems(parts * (n - 1)), sems(parts * (n - 1)),
+            sems(1), sems(n - 1), sems(n - 1), sems(n),
+            pltpu.SemaphoreType.DMA((2, 2, nz - 1)),
+            pltpu.SemaphoreType.DMA(()),
         ],
         compiler_params=pltpu.CompilerParams(
-            collective_id=1, has_side_effects=True, vmem_limit_bytes=VMEM_LIMIT
+            collective_id=0, has_side_effects=True, vmem_limit_bytes=VMEM_LIMIT
         ),
-        cost_estimate=pl.CostEstimate(flops=20 * fft_flops, bytes_accessed=64 * channels * positions, transcendentals=0),
-        name="backward",
-    )(query_proj[0], key_proj[0], value_proj[0], out_weight, pieces, conv, fspec, *tables)
+        cost_estimate=pl.CostEstimate(
+            flops=60 * parts * spec_rows * 256 * 256 + 4 * channels * features * positions,
+            bytes_accessed=64 * channels * positions, transcendentals=0,
+        ),
+        name="hyena",
+    )(query_proj[0], key_proj[0], value_proj[0], grad_out[0], out_weight, long_filter, *tables)
     return (grad_query[None], grad_key[None], grad_value[None], grad_weight.astype(f32))
 
 

time: 128 us -> 102 us (0.80)
  between operations: 14.1 us -> 0.66 us
  waiting for transfers between devices: 12.2 us -> 0 us
    all_gather x1 -> x0, waiting for transfers between devices: 11.6 us -> none  [shards(): pieces = lax.all_gather(grad_out[0], 'chan', axis=0, tiled=True)]
    pallas_call x2 -> x1, Pallas kernels: 95.4 us -> 94.7 us  [shards(): pl.pallas_call(functools.partial(kernel, n, nz, parts, scale), out_shape=...]
  transfers between devices with their start and end apart: 1 -> 0, of which waited for: 1 -> 0; matrix products, arithmetic and copies ran while one was open for 0% -> 0% of each run, Pallas kernels for 30% -> 0%
where the time goes in v2:
time: 102 us
  Pallas kernels  94.7 us (93%)
  other arithmetic  4.22 us (4%)
  local copies, waits for them, and re-layouts  2.39 us (2%)
    pallas_call x1, Pallas kernels, shards(): pl.pallas_call(functools.partial(kernel, n, nz, parts, scale), out_shape=...  94.7 us
    convert_element_type x1, other arithmetic, shards(): grad_weight.astype(f32)  4.22 us
    unnamed x9, local copies, waits for them, and re-layouts  2.39 us

profile of v2, /device:TPU:0, one launch (start us, length us, event | category | flops | bytes accessed | tf_op | source)
XLA Modules:
  0.0 102.0 jit_solution(11573314772993362876)
XLA Ops:
  0.6 94.7 %hyena.1 = (bf16[512,512]{1,0:T(8,128)(2,1)}, bf16[512,512]{1,0:T(8,128)(2,1)}, bf16[512,512]{1,0:T(8,128)(2,1)}, bf16[512,2048]{1,0:T(8,128)(2,1)}) custom-call(bf16[512,512]{1,0:T(8,128)(2,1)} %bitcast.10, bf16[512,512]{1,0:T(8,128)(2,1)} %bitcast.11, bf16[512,512]{1,0:T(8,128)(2,1)} %bitcast.12, bf16[512,512]{1,0:T(8,128)(2,1)} %bitcast.13, ...), custom_call_target="tpu_custom_call" | custom-call | flops 10703863808 | bytes 16777216 | tf_op jit(solution)/shard_map/hyena/pallas_call | solution.py:397
  95.3 0.0 copy-start.2
  95.4 0.0 copy-start.1
  95.4 4.2 %convert_element_type.3 = f32[512,2048]{1,0:T(8,128)} convert(bf16[512,2048]{1,0:T(8,128)(2,1)} %get-tuple-element.11) | non-fusion elementwise | flops 1048576 | bytes 6291456 | tf_op jit(solution)/shard_map/convert_element_type | solution.py:428
  99.6 0.0 copy-done.2
  99.6 0.0 copy-start
  99.6 0.8 copy.19
  100.4 0.0 copy-done.1
  100.4 0.8 copy.20
  101.2 0.0 copy-done
  101.2 0.8 copy.21
Async XLA Ops:
  95.3 4.2 %copy-start.2 = (bf16[512,512]{1,0:T(8,128)(2,1)S(1)}, bf16[512,512]{1,0:T(8,128)(2,1)}, u32[]{:S(2)}) copy-start(bf16[512,512]{1,0:T(8,128)(2,1)} %get-tuple-element.8) | copy-start | bytes 1572868
  95.4 5.0 %copy-start.1 = (bf16[512,512]{1,0:T(8,128)(2,1)S(1)}, bf16[512,512]{1,0:T(8,128)(2,1)}, u32[]{:S(2)}) copy-start(bf16[512,512]{1,0:T(8,128)(2,1)} %get-tuple-element.9) | copy-start | bytes 1572868
  99.6 1.6 %copy-start = (bf16[512,512]{1,0:T(8,128)(2,1)S(1)}, bf16[512,512]{1,0:T(8,128)(2,1)}, u32[]{:S(2)}) copy-start(bf16[512,512]{1,0:T(8,128)(2,1)} %get-tuple-element.10) | copy-start | bytes 1572868

commit v3 on v2

--- a/solution.py
+++ b/solution.py
@@ -235,10 +235,8 @@
         )
         pl.when((origin >= 0) & (origin < nz))(copy.wait_recv)
 
-    direct = min(2, nz - 1)
-    for distance in range(direct, 0, -1):
-        for side in range(2):
-            line_start(side, distance, distance)
+    for side in range(2):
+        line_start(side, 1, 1)
     keep = pltpu.make_async_copy(own_ref, pieces.at[piece_ids(level)], own_sem)
     keep.start()
 
@@ -288,18 +286,17 @@
             copy.wait()
         convolve(full, h, False)
         home.extend(come_home(full, conv, conv_sems, h))
-    for distance in range(3, nz):
-        for side in range(2):
-            line_arrived(side, distance - 1)
-            line_start(side, distance, 1)
+        for distance in range(2 + h, nz if h == parts - 1 else min(3 + h, nz)):
+            for side in range(2):
+                line_arrived(side, distance - 1)
+                line_start(side, distance, 1)
     for copy in home:
         copy.wait()
     keep.wait()
     for side in range(2):
+        line_arrived(side, nz - 1)
         for distance in range(1, nz):
-            if not 2 <= distance < nz - 1:
-                line_arrived(side, distance)
-            line_sent(side, distance, distance if distance <= direct else 1)
+            line_sent(side, distance, 1)
 
     out = [[] for _ in range(parts)]
     for slot, p in enumerate(peers + [me]):
@@ -382,7 +379,7 @@
     local = positions // LANES
     slabs, width = local * n, channels // n
     nz = lax.axis_size("chan")
-    parts = 2
+    parts = 2 if width % 32 == 0 else 1
     part_width = width // parts
     spec_rows = (slabs + 1) * part_width
     features = out_weight.shape[1]

time: 102 us -> 101 us (level)
  no operation moved by 1% of the time
where the time goes in v3:
time: 101 us
  Pallas kernels  93.9 us (93%)
  other arithmetic  4.22 us (4%)
  local copies, waits for them, and re-layouts  2.39 us (2%)
    pallas_call x1, Pallas kernels, shards(): pl.pallas_call(functools.partial(kernel, n, nz, parts, scale), out_shape=...  93.9 us
    convert_element_type x1, other arithmetic, shards(): grad_weight.astype(f32)  4.22 us
    unnamed x9, local copies, waits for them, and re-layouts  2.39 us

profile of v3, /device:TPU:0, one launch (start us, length us, event | category | flops | bytes accessed | tf_op | source)
XLA Modules:
  0.0 101.2 jit_solution(12779795517601900260)
XLA Ops:
  0.6 93.9 %hyena.1 = (bf16[512,512]{1,0:T(8,128)(2,1)}, bf16[512,512]{1,0:T(8,128)(2,1)}, bf16[512,512]{1,0:T(8,128)(2,1)}, bf16[512,2048]{1,0:T(8,128)(2,1)}) custom-call(bf16[512,512]{1,0:T(8,128)(2,1)} %bitcast.10, bf16[512,512]{1,0:T(8,128)(2,1)} %bitcast.11, bf16[512,512]{1,0:T(8,128)(2,1)} %bitcast.12, bf16[512,512]{1,0:T(8,128)(2,1)} %bitcast.13, ...), custom_call_target="tpu_custom_call" | custom-call | flops 10703863808 | bytes 16777216 | tf_op jit(solution)/shard_map/hyena/pallas_call | solution.py:394
  94.5 0.0 copy-start.2
  94.5 0.0 copy-start.1
  94.5 4.2 %convert_element_type.3 = f32[512,2048]{1,0:T(8,128)} convert(bf16[512,2048]{1,0:T(8,128)(2,1)} %get-tuple-element.11) | non-fusion elementwise | flops 1048576 | bytes 6291456 | tf_op jit(solution)/shard_map/convert_element_type | solution.py:425
  98.8 0.0 copy-done.2
  98.8 0.0 copy-start
  98.8 0.8 copy.19
  99.6 0.0 copy-done.1
  99.6 0.8 copy.20
  100.4 0.0 copy-done
  100.4 0.8 copy.21
Async XLA Ops:
  94.5 4.2 %copy-start.2 = (bf16[512,512]{1,0:T(8,128)(2,1)S(1)}, bf16[512,512]{1,0:T(8,128)(2,1)}, u32[]{:S(2)}) copy-start(bf16[512,512]{1,0:T(8,128)(2,1)} %get-tuple-element.8) | copy-start | bytes 1572868
  94.5 5.0 %copy-start.1 = (bf16[512,512]{1,0:T(8,128)(2,1)S(1)}, bf16[512,512]{1,0:T(8,128)(2,1)}, u32[]{:S(2)}) copy-start(bf16[512,512]{1,0:T(8,128)(2,1)} %get-tuple-element.9) | copy-start | bytes 1572868
  98.8 1.6 %copy-start = (bf16[512,512]{1,0:T(8,128)(2,1)S(1)}, bf16[512,512]{1,0:T(8,128)(2,1)}, u32[]{:S(2)}) copy-start(bf16[512,512]{1,0:T(8,128)(2,1)} %get-tuple-element.10) | copy-start | bytes 1572868
